TPU v7x, 128 devices: a whole 4x4x4 slice. The times are simulated.
128 devices in a mesh: ao: 16 (over y_hi, x, core), aux: 4 (over z), occ: 2 (over y_lo).
Axes of the slice: x: 4, y: 4 (y_hi: 2, y_lo: 2; y = y_hi * 2 + y_lo), z: 4, core: 2. Of those that a mesh axis runs over, the one named last changes fastest.
Arguments:
- half_factors: bfloat16 [1536, 8, 8192], P('aux', 'occ', 'ao'), may hold values from -0.56640625 to 0.56640625
Outputs:
- exchange_matrix: float32 [8192, 8192], P('ao', ('aux', 'occ'))
All inputs are finite; a program needn't handle non-finite values.
Results may differ from a plain program's by a relative error of at most 0.0003.
Values may be sent and summed in bfloat16 or wider, within the bound.
A program may use at most 128 MiB of HBM per device.

v0:
```python
import jax
import jax.numpy as jnp
from jax import lax
from jax.sharding import PartitionSpec as P


def contract(local_rows, visitor):
    return lax.dot_general(
        local_rows, visitor, (((0,), (0,)), ((), ())), preferred_element_type=jnp.float32
    )


def on_device(half_factors):
    block_rows = half_factors.shape[2]
    local_rows = half_factors.reshape(-1, block_rows)
    shard_piece = lax.all_gather(half_factors, "ao", axis=2, tiled=True)
    visitor = shard_piece.reshape(-1, shard_piece.shape[2])
    partial_value = contract(local_rows, visitor)
    return lax.psum_scatter(partial_value, ("aux", "occ"), scatter_dimension=1, tiled=True)


def solution(mesh):
    placed = (P("aux", "occ", "ao"),)
    return jax.shard_map(
        on_device, mesh=mesh, in_specs=placed, out_specs=P("ao", ("aux", "occ")), check_vma=False
    )
```

profile of v0, /device:TPU:33, one launch (start us, length us, event | category | flops | bytes accessed | tf_op | source)
XLA Modules:
  0.0 531.9 jit_solution(575805945294478686)
XLA Ops:
  6.5 0.0 copy-start
  6.5 0.0 all-gather.2.cloned.1.call-start
  6.5 3.0 copy.2
  9.5 0.0 all-gather.2.cloned.1.call-update
  9.5 0.0 reduce-scatter.2.cloned.1.call-start
  9.6 169.3 %all-gather.2.cloned.1.call-done = bf16[384,4,8192]{2,0,1:T(8,128)(2,1)} async-done(((bf16[384,4,512]{2,0,1:T(8,128)(2,1)}), bf16[384,4,8192]{2,0,1:T(8,128)(2,1)}) %all-gather.2.cloned.1.call-update) | async-done | bytes 25165840 | tf_op jit(solution)/shard_map/all_gather | solution.py:16
  178.9 0.0 copy-done
  178.9 22.2 %convolution_bitcast_fusion = f32[512,8192]{1,0:T(8,128)} fusion(bf16[384,4,8192]{2,0,1:T(8,128)(2,1)} %all-gather.2.cloned.1.call-done, bf16[384,4,512]{2,1,0:T(4,128)(2,1)S(1)} %copy-done), kind=kOutput, calls=%fused_computation | convolution fusion | flops 12884901888 | bytes 43515904 | tf_op jit(solution)/shard_map/dot_general | solution.py:8
  201.1 0.0 reduce-scatter.2.cloned.1.call-update
  201.1 324.0 %reduce-scatter.2.cloned.1.call-done = f32[512,1024]{1,0:T(8,128)} async-done(((f32[512,8192]{1,0:T(8,128)}), f32[512,1024]{1,0:T(8,128)}) %reduce-scatter.2.cloned.1.call-update) | async-done | bytes 2097168 | tf_op jit(solution)/shard_map/reduce_scatter | solution.py:19
Async XLA Ops:
  6.5 172.3 %copy-start = (bf16[384,4,512]{2,1,0:T(4,128)(2,1)S(1)}, bf16[384,4,512]{2,1,0:T(4,128)(2,1)}, u32[]{:S(2)}) copy-start(bf16[384,4,512]{2,1,0:T(4,128)(2,1)} %param.1) | copy-start | bytes 4718596
  6.5 172.3 %all-gather.2.cloned.1.call-start = ((), (), s32[]{:S(2)}) async-start(), calls=%async_computation.1 | async-start | bytes 26738688 | tf_op jit(solution)/shard_map/all_gather | solution.py:16
  9.5 515.5 %reduce-scatter.2.cloned.1.call-start = ((), (), s32[]{:S(2)}) async-start(), calls=%async_computation.2 | async-start | bytes 18874368 | tf_op jit(solution)/shard_map/reduce_scatter | solution.py:19
Sparse Core Ops, SparseCore 0:
  9.7 169.1 all-gather.1
  201.2 323.7 reduce-scatter.1
where the time goes:
time: 533 us; the launch traced here: 532 us
  waiting for transfers between devices  493 us (92%)
  matrix products  22.2 us (4%)
  between operations  13.4 us (3%)
    reduce_scatter x1, waiting for transfers between devices, on_device(): lax.psum_scatter(partial_value, ('aux', 'occ'), scatter_dimension=1, tile...  324 us
    all_gather x1, waiting for transfers between devices, on_device(): shard_piece = lax.all_gather(half_factors, 'ao', axis=2, tiled=True)  169 us
    dot_general x1, matrix products, contract(): lax.dot_general(local_rows, visitor, (((0,), (0,)), ((), ())), preferred_...  22.2 us
  transfers between devices with their start and end apart: 2, of which 2 were waited for; matrix products, arithmetic and copies ran while one was open for 0% of the time, Pallas kernels for 0%

commit v1 on v0

v1 whole, which is shorter than its diff:
```python
import jax
import jax.numpy as jnp
from jax import lax
from jax.experimental import pallas as pl
from jax.experimental.pallas import tpu as pltpu
from jax.sharding import PartitionSpec as P

MESH = pl.DeviceIdType.MESH
DEPTH, LANES, BLOCK = 1536, 128, 512
D, E, B, A, C = range(5)
ODD = (True, True, False, False, False)
MIRRORED = (True, True, True, False, False)


def kernel(d_ref, out_ref, own, cp, r, rt, p, ha, fu, fint, own_sem, cp_sem, ysend, yrecv, xsend, xrecv, csend, crecv,
           hsend, hrecv, usend, urecv, fsend, msend, frecv):
    ao, z, yl = lax.axis_index("ao"), lax.axis_index("aux"), lax.axis_index("occ")
    c, x, y = ao % 2, (ao // 2) % 4, (ao // 8) * 2 + yl

    def at(x, y, z, c):
        return ((y // 2) * 8 + x * 2 + c, z, y % 2)

    def near(dx=0, dy=0, dz=0, dc=0):
        return at((x + dx) % 4, (y + dy) % 4, (z + dz) % 4, (c + dc) % 2)

    def remote(src, dst, send, recv, device):
        return pltpu.make_async_remote_copy(
            src_ref=src, dst_ref=dst, send_sem=send, recv_sem=recv, device_id=device, device_id_type=MESH
        )

    load = pltpu.make_async_copy(d_ref, own, own_sem)
    load.start()

    mx, mz = (z % 2) * 2 + y % 2, (y // 2) * 2 + x // 2
    here = jnp.logical_and(mx == x, mz == z)
    barrier = pltpu.get_barrier_semaphore()
    for device in (near(dx=1), near(dx=3), near(dz=1), near(dz=3), near(dc=1), near(dy=1), near(dy=2), near(dy=3)):
        pl.semaphore_signal(barrier, inc=1, device_id=device, device_id_type=MESH)
    for my in range(4):
        for mc in range(2):
            @pl.when(jnp.logical_not(here & (y == my) & (c == mc)))
            def _():
                pl.semaphore_signal(barrier, inc=1, device_id=at(mx, my, mz, mc), device_id_type=MESH)
    pl.semaphore_wait(barrier, 16 - here.astype(jnp.int32))
    load.wait()

    sends = []

    def go(copy):
        copy.start()
        sends.append(copy)

    def piece(jx, jy):
        return cp.at[(x + jx) % 4, c, (y + jy) % 4]

    def to_core(src, jx, jy):
        go(remote(src, piece(jx, jy), csend.at[jx, jy], crecv.at[jx, jy], near(dc=1)))

    def to_x(src, jy):
        go(remote(src, piece(0, jy), xsend.at[0, jy], xrecv.at[3, jy], near(dx=1)))
        go(remote(src, piece(0, jy), xsend.at[1, jy], xrecv.at[1, jy], near(dx=3)))

    def wait_y(j, ds):
        dst = piece(0, j) if ds == 0 else r.at[j - 1, ds - 1]
        remote(dst, dst, ysend.at[0, 0], yrecv.at[j, ds], near(dy=1)).wait_recv()

    def wait_x(jx, jy):
        dst = piece(jx, jy)
        remote(dst, dst, xsend.at[0, 0], xrecv.at[jx, jy], near(dx=1)).wait_recv()
        to_core(dst, jx, jy)

    def wait_core(jx):
        for jy in range(4):
            dst = cp.at[(x + jx) % 4, 1 - c, (y + jy) % 4]
            remote(dst, dst, csend.at[0, 0], crecv.at[jx, jy], near(dc=1)).wait_recv()

    mine = own.at[y]
    go(remote(own.at[(y + 1) % 4], cp.at[x, c, y], ysend.at[0, 0], yrecv.at[3, 0], near(dy=1)))
    go(remote(own.at[(y + 3) % 4], cp.at[x, c, y], ysend.at[1, 0], yrecv.at[1, 0], near(dy=3)))
    to_x(mine, 0)
    to_core(mine, 0, 0)
    keep = pltpu.make_async_copy(mine, piece(0, 0), cp_sem)
    keep.start()
    go(remote(own.at[(y + 2) % 4], r.at[2, 0], ysend.at[0, 1], yrecv.at[3, 1], near(dy=1)))
    go(remote(mine, r.at[0, 0], ysend.at[1, 1], yrecv.at[1, 1], near(dy=3)))

    wait_y(3, 0)
    to_x(piece(0, 3), 3)
    to_core(piece(0, 3), 0, 3)
    wait_y(1, 0)
    to_x(piece(0, 1), 1)
    to_core(piece(0, 1), 0, 1)
    go(remote(piece(0, 1), r.at[1, 0], ysend.at[1, 2], yrecv.at[2, 1], near(dy=3)))
    wait_x(1, 0)
    wait_x(3, 0)
    wait_y(3, 1)
    go(remote(r.at[2, 0], piece(0, 3), ysend.at[0, 2], yrecv.at[2, 0], near(dy=1)))
    go(remote(own.at[(y + 3) % 4], r.at[2, 1], ysend.at[0, 3], yrecv.at[3, 2], near(dy=1)))
    wait_y(1, 1)
    go(remote(own.at[(y + 1) % 4], r.at[0, 1], ysend.at[1, 3], yrecv.at[1, 2], near(dy=3)))
    go(remote(r.at[0, 0], r.at[1, 1], ysend.at[1, 4], yrecv.at[2, 2], near(dy=3)))
    wait_x(1, 3)
    wait_x(3, 3)
    wait_y(2, 0)
    to_x(piece(0, 2), 2)
    to_core(piece(0, 2), 0, 2)
    wait_x(1, 1)
    wait_x(3, 1)
    keep.wait()

    def pass_x(jx, jy, k):
        go(remote(piece(jx, jy), piece(jx, jy), xsend.at[k, jy + 4], xrecv.at[2, jy], near(dx=4 - jx)))

    pass_x(3, 0, 0)
    pass_x(1, 3, 1)

    def turn(ds):
        for j in range(4):
            yy = (y + j) % 4
            if ds == 0:
                block = cp[x, c, yy]
            elif j == 0:
                block = own[(y + ds) % 4]
            else:
                block = r[j - 1, ds - 1]
            rt[ds, yy] = block.T

    wait_y(2, 1)
    turn(1)
    turn(0)
    wait_x(1, 2)
    wait_x(3, 2)
    pass_x(3, 2, 0)
    pass_x(1, 1, 1)
    wait_core(0)
    wait_core(1)
    wait_core(3)

    def which(g, q):
        if ODD[g]:
            xp = jnp.where(q == x // 2, x ^ 1, 3 - x)
            ds = jnp.where(xp == (x + 1) % 4, 0, 2) if g == E else 1
        else:
            xp = jnp.where(q == x // 2, x, (x + 2) % 4)
            ds = (None, None, 1, 0, 2)[g]
        return xp, ds

    def rise(g):
        @pl.loop(0, 4)
        def _(i):
            j = (i + 2) % 4
            d = (z + j) % 4
            xp, ds = which(g, d % 2)
            for yh in range(2):
                total = None
                for k in range(2):
                    lhs = rt[ds, 2 * yh + k]
                    rhs = jnp.concatenate([cp[xp, 0, 2 * (d // 2) + k], cp[xp, 1, 2 * (d // 2) + k]], axis=1)
                    part = jnp.dot(lhs, rhs, preferred_element_type=jnp.float32)
                    total = part if total is None else total + part
                p[g, j, yh] = total

        go(remote(p.at[g, 2, 0], ha.at[g, 0], hsend.at[g, 0], hrecv.at[g, 0], near(dz=3)))
        go(remote(p.at[g, 2, 1], ha.at[g, 1], hsend.at[g, 1], hrecv.at[g, 1], near(dz=1)))
        go(remote(p.at[g, 3, 1], fu.at[g, 0, 1], usend.at[g, 0, 1], urecv.at[g, 0, 1], near(dz=3)))
        go(remote(p.at[g, 1, 0], fu.at[g, 1, 0], usend.at[g, 1, 0], urecv.at[g, 1, 0], near(dz=1)))

    def middle(g):
        for k, j in ((0, 3), (1, 1)):
            remote(ha.at[g, k], ha.at[g, k], hsend.at[g, k], hrecv.at[g, k], near(dz=1)).wait_recv()
            p[g, j, k] += ha[g, k]
            go(remote(p.at[g, j, k], fu.at[g, k, k], usend.at[g, k, k], urecv.at[g, k, k], near(dz=j)))

    checks = []

    def deliver(src, dst, sem, device, same):
        @pl.when(jnp.logical_not(same))
        def _():
            remote(src, dst, sem, frecv, device).start()

        @pl.when(same)
        def _():
            pltpu.make_async_copy(src, dst, frecv).start()

        checks.append((src, dst, sem, device, same))

    def finish(g):
        for k in range(2):
            for h in range(2):
                remote(fu.at[g, k, h], fu.at[g, k, h], usend.at[g, k, h], urecv.at[g, k, h], near(dz=1)).wait_recv()
        xp, ds = which(g, z % 2)
        s = (y + ds) % 4
        for yh in range(2):
            value = p[g, 0, yh] + fu[g, 0, yh] + fu[g, 1, yh]
            p[g, 0, yh] = value
            if MIRRORED[g]:
                for cc in range(2):
                    fint[g, cc, yh] = value[:, cc * LANES:(cc + 1) * LANES].T
        for yh in range(2):
            for cc in range(2):
                yy = yh * 2 + xp % 2
                deliver(
                    p.at[g, 0, yh, :, pl.ds(cc * LANES, LANES)],
                    out_ref.at[pl.ds(pl.multiple_of(s * LANES, LANES), LANES),
                               pl.ds(pl.multiple_of(cc * BLOCK + y * LANES, LANES), LANES)],
                    fsend.at[g, yh, cc], at(x, yy, z, c), yy == y,
                )
                if MIRRORED[g]:
                    yy, zz = (z // 2) * 2 + x % 2, yh * 2 + x // 2
                    same = (xp == x) & (yy == y) & (zz == z) & (c == cc)
                    deliver(
                        fint.at[g, cc, yh],
                        out_ref.at[pl.ds(pl.multiple_of(y * LANES, LANES), LANES),
                                   pl.ds(pl.multiple_of(c * BLOCK + s * LANES, LANES), LANES)],
                        msend.at[g, yh, cc], at(xp, yy, zz, cc), same,
                    )

    rise(D)
    wait_y(3, 2)
    wait_y(1, 2)
    wait_y(2, 2)
    turn(2)
    rise(E)
    middle(D)
    for jy in (0, 3, 1, 2):
        wait_x(2, jy)
    middle(E)
    wait_core(2)
    rise(B)
    finish(D)
    rise(A)
    middle(B)
    finish(E)
    rise(C)
    middle(A)
    finish(B)
    middle(C)
    finish(A)
    finish(C)

    for copy in sends:
        copy.wait_send()
    for src, dst, sem, device, same in checks:
        @pl.when(jnp.logical_not(same))
        def _():
            remote(src, dst, sem, frecv, device).wait_send()
    pltpu.make_async_copy(out_ref, out_ref, frecv).wait()


def on_device(half_factors):
    d = half_factors.reshape(DEPTH, 4, LANES).transpose(1, 0, 2)
    dma = pltpu.SemaphoreType.DMA
    bf16, f32 = jnp.bfloat16, jnp.float32
    return pl.pallas_call(
        kernel,
        out_shape=jax.ShapeDtypeStruct((BLOCK, 2 * BLOCK), f32),
        in_specs=[pl.BlockSpec(memory_space=pl.ANY)],
        out_specs=pl.BlockSpec(memory_space=pl.ANY),
        scratch_shapes=[
            pltpu.VMEM((4, DEPTH, LANES), bf16),
            pltpu.VMEM((4, 2, 4, DEPTH, LANES), bf16),
            pltpu.VMEM((3, 2, DEPTH, LANES), bf16),
            pltpu.VMEM((3, 4, LANES, DEPTH), bf16),
            pltpu.VMEM((5, 4, 2, LANES, 2 * LANES), f32),
            pltpu.VMEM((5, 2, LANES, 2 * LANES), f32),
            pltpu.VMEM((5, 2, 2, LANES, 2 * LANES), f32),
            pltpu.VMEM((3, 2, 2, LANES, LANES), f32),
            dma, dma, dma((2, 5)), dma((4, 3)), dma((2, 8)), dma((4, 4)), dma((4, 4)), dma((4, 4)),
            dma((5, 2)), dma((5, 2)), dma((5, 2, 2)), dma((5, 2, 2)), dma((5, 2, 2)), dma((3, 2, 2)), dma,
        ],
        name="exchange",
        cost_estimate=pl.CostEstimate(flops=2 * 10 * 256 * 512 * 3072, bytes_accessed=4 << 20, transcendentals=0),
        compiler_params=pltpu.CompilerParams(collective_id=0, has_side_effects=True, vmem_limit_bytes=48 << 20),
    )(d)


def solution(mesh):
    return jax.shard_map(
        on_device, mesh=mesh, in_specs=(P("aux", "occ", "ao"),), out_specs=P("ao", ("aux", "occ")), check_vma=False
    )
```

time: 533 us -> 152 us (0.29)
  waiting for transfers between devices: 493 us -> 0 us
  Pallas kernels: 0 us -> 148 us
  matrix products: 22.2 us -> 0 us
  between operations: 13.4 us -> 0.02 us
    reduce_scatter x1 -> x0, waiting for transfers between devices: 324 us -> none  [on_device(): lax.psum_scatter(partial_value, ('aux', 'occ'), scatter_dimension=1, tile...]
    all_gather x1 -> x0, waiting for transfers between devices: 169 us -> none  [on_device(): shard_piece = lax.all_gather(half_factors, 'ao', axis=2, tiled=True)]
    pallas_call x0 -> x1, Pallas kernels: none -> 148 us  [on_device(): pl.pallas_call(kernel, out_shape=jax.ShapeDtypeStruct((BLOCK, 2 * BLOCK),...]
    dot_general x1 -> x0, matrix products: 22.2 us -> none  [contract(): lax.dot_general(local_rows, visitor, (((0,), (0,)), ((), ())), preferred_...]
  transfers between devices with their start and end apart: 2 -> 0, of which waited for: 2 -> 0; matrix products, arithmetic and copies ran while one was open for 0% -> 0% of each run, Pallas kernels for 0% -> 0%
where the time goes in v1:
time: 152 us
  Pallas kernels  148 us (97%)
  local copies, waits for them, and re-layouts  4.02 us (3%)
    pallas_call x1, Pallas kernels, on_device(): pl.pallas_call(kernel, out_shape=jax.ShapeDtypeStruct((BLOCK, 2 * BLOCK),...  148 us

profile of v1, /device:TPU:33, one launch (start us, length us, event | category | flops | bytes accessed | tf_op | source)
XLA Modules:
  0.0 152.0 jit_solution(2984474243640281669)
XLA Ops:
  0.0 2.5 %reshape.3 = bf16[1536,4,128]{2,1,0:T(4,128)(2,1)S(1)} reshape(bf16[384,4,512]{2,1,0:T(4,128)(2,1)} %param.1) | data formatting | bytes 3145728 | tf_op jit(solution)/shard_map/reshape | solution.py:251
  2.5 0.2 copy.4
  2.7 148.0 %exchange.1 = f32[512,1024]{1,0:T(8,128)S(1)} custom-call(bf16[4,1536,128]{2,1,0:T(8,128)(2,1)S(1)} %bitcast.3), custom_call_target="tpu_custom_call" | custom-call | flops 8053063680 | bytes 4194304 | tf_op jit(solution)/shard_map/exchange/pallas_call | solution.py:254
  150.7 1.3 copy.6

commit v2 on v0

v2 whole, which is shorter than its diff:
```python
import jax
import jax.numpy as jnp
from jax import lax
from jax.experimental import pallas as pl
from jax.experimental.pallas import tpu as pltpu
from jax.sharding import PartitionSpec as P

MESH = pl.DeviceIdType.MESH
DEPTH, LANES, BLOCK = 1536, 128, 512
HALF = DEPTH // 2
WIDE = 2 * LANES
PRODUCTS = (
    (0, 1, 0), (0, 0, None), (1, 1, 1), (3, 1, 1), (1, 0, 2), (3, 2, 2), (0, 2, None), (2, 1, 0), (2, 2, None), (2, 0, None)
)


def kernel(d_ref, out_ref, own, cp, r, rt, p, ha, fu, fint, mb, own_sem, keep_sem, ysend, yrecv, xsend, xrecv, csend, crecv,
           hsend, hrecv, usend, urecv, fsend, msend, mrecv, gsend, frecv):
    ao, z, yl = lax.axis_index("ao"), lax.axis_index("aux"), lax.axis_index("occ")
    c, x, y = ao % 2, (ao // 2) % 4, (ao // 8) * 2 + yl

    def at(x, y, z, c):
        return ((y // 2) * 8 + x * 2 + c, z, y % 2)

    def near(dx=0, dy=0, dz=0, dc=0):
        return at((x + dx) % 4, (y + dy) % 4, (z + dz) % 4, (c + dc) % 2)

    def remote(src, dst, send, recv, device):
        return pltpu.make_async_remote_copy(
            src_ref=src, dst_ref=dst, send_sem=send, recv_sem=recv, device_id=device, device_id_type=MESH
        )

    load = pltpu.make_async_copy(d_ref, own, own_sem)
    load.start()

    here = x // 2 == z % 2
    barrier = pltpu.get_barrier_semaphore()
    for device in (near(dx=1), near(dx=3), near(dz=1), near(dz=3), near(dc=1), near(dy=1), near(dy=2), near(dy=3)):
        pl.semaphore_signal(barrier, inc=1, device_id=device, device_id_type=MESH)
    for bx in range(2):
        for bz in range(2):
            for mc in range(2):
                mx, mz = (z % 2) * 2 + bx, bz * 2 + x // 2

                @pl.when(jnp.logical_not((mx == x) & (mz == z) & (mc == c)))
                def _():
                    pl.semaphore_signal(barrier, inc=1, device_id=at(mx, y, mz, mc), device_id_type=MESH)
    pl.semaphore_wait(barrier, 16 - here.astype(jnp.int32))
    load.wait()

    sends = []

    def go(copy):
        copy.start()
        sends.append(copy)

    def piece(jx, jy, h):
        return cp.at[(x + jx) % 4, c, (y + jy) % 4, h]

    def mine(ds, h):
        return own.at[(y + ds) % 4, h]

    def to_core(src, jx, jy, h):
        go(remote(src, piece(jx, jy, h), csend.at[jx, jy, h], crecv.at[jx, jy, h], near(dc=1)))

    def to_x(src, jy, h):
        go(remote(src, piece(0, jy, h), xsend.at[0, jy, h], xrecv.at[3, jy, h], near(dx=1)))
        go(remote(src, piece(0, jy, h), xsend.at[1, jy, h], xrecv.at[1, jy, h], near(dx=3)))
        to_core(src, 0, jy, h)

    def to_y(src, dst, k, n, j, ds, h):
        go(remote(src, dst, ysend.at[k, n, h], yrecv.at[j, ds, h], near(dy=1 + 2 * k)))

    def wait_y(j, ds, h):
        dst = piece(0, j, h) if ds == 0 else r.at[j - 1, ds - 1, h]
        remote(dst, dst, ysend.at[0, 0, 0], yrecv.at[j, ds, h], near(dy=1)).wait_recv()

    def wait_x(jx, jy, h):
        dst = piece(jx, jy, h)
        remote(dst, dst, xsend.at[0, 0, 0], xrecv.at[jx, jy, h], near(dx=1)).wait_recv()
        to_core(dst, jx, jy, h)

    def pass_x(jx, jy, h):
        k = 0 if jx == 3 else 1
        dst = piece(jx, jy, h)
        go(remote(dst, dst, xsend.at[k, jy + 4, h], xrecv.at[2, jy, h], near(dx=4 - jx)))

    def wait_core(jx, jy, h):
        dst = cp.at[(x + jx) % 4, 1 - c, (y + jy) % 4, h]
        remote(dst, dst, csend.at[0, 0, 0], crecv.at[jx, jy, h], near(dc=1)).wait_recv()

    keeps = []
    for h in range(2):
        to_y(mine(3, h), piece(0, 0, h), 1, 0, 1, 0, h)
        to_y(mine(2, h), r.at[2, 0, h], 0, 1, 3, 1, h)
        to_x(mine(0, h), 0, h)
    for h in range(2):
        to_y(mine(0, h), r.at[0, 0, h], 1, 1, 1, 1, h)
        to_y(mine(1, h), piece(0, 0, h), 0, 0, 3, 0, h)
        keeps.append(pltpu.make_async_copy(mine(0, h), piece(0, 0, h), keep_sem.at[h]))
        keeps[h].start()
    for h in range(2):
        wait_y(1, 0, h)
        to_x(piece(0, 1, h), 1, h)
        wait_y(3, 1, h)
        to_y(r.at[2, 0, h], piece(0, 3, h), 0, 2, 2, 0, h)
        to_y(piece(0, 1, h), r.at[1, 0, h], 1, 2, 2, 1, h)
        wait_x(1, 0, h)
        wait_x(3, 0, h)
    for h in range(2):
        wait_y(3, 0, h)
        to_x(piece(0, 3, h), 3, h)
        wait_y(1, 1, h)
        wait_x(1, 1, h)
        wait_x(3, 1, h)
    for h in range(2):
        to_y(mine(3, h), r.at[2, 1, h], 0, 3, 3, 2, h)
        to_y(mine(1, h), r.at[0, 1, h], 1, 3, 1, 2, h)
    for h in range(2):
        to_y(r.at[0, 0, h], r.at[1, 1, h], 1, 4, 2, 2, h)
    for h in range(2):
        wait_y(2, 0, h)
        to_x(piece(0, 2, h), 2, h)
    for h in range(2):
        pass_x(3, 0, h)
        pass_x(1, 1, h)

    def turn(ds):
        for j in range(4):
            yy = (y + j) % 4
            for h in range(2):
                if ds == 0:
                    block = cp[x, c, yy, h]
                elif j == 0:
                    block = own[(y + ds) % 4, h]
                else:
                    block = r[j - 1, ds - 1, h]
                rows = pl.ds(pl.multiple_of((yy // 2) * LANES, LANES), LANES)
                rt[ds, yy % 2, rows, pl.ds(h * HALF, HALF)] = block.T

    def rows(k):
        return pl.ds(k * LANES, LANES)

    def role(b):
        dx, ds, keep = PRODUCTS[b]
        xp = (x + dx) % 4
        return xp, ds, keep, z % 2 == xp // 2

    def rise(b):
        xp, ds, _, even = role(b)
        far = 1 - z // 2

        @pl.loop(0, 2)
        def _(i):
            u = (far + i) % 2
            total = None
            for k in range(2):
                rhs = jnp.concatenate([cp[xp, cc, 2 * u + k].reshape(DEPTH, LANES) for cc in range(2)], axis=1)
                part = jnp.dot(rt[ds, k], rhs, preferred_element_type=jnp.float32)
                total = part if total is None else total + part
            p[b, u] = total

        @pl.when(even)
        def _():
            for k in range(2):
                remote(p.at[b, far, rows(k)], ha.at[b, k], hsend.at[b, k], hrecv.at[b, k], near(dz=3 - 2 * k)).start()

        @pl.when(jnp.logical_not(even))
        def _():
            for k in range(2):
                u = ((z + 3 - 2 * k) % 4) // 2
                remote(p.at[b, u, rows(1 - k)], fu.at[b, k, rows(1 - k)], usend.at[b, k, 0], urecv.at[b, k, 0],
                       near(dz=3 - 2 * k)).start()

    def middle(b):
        _, _, _, even = role(b)

        @pl.when(jnp.logical_not(even))
        def _():
            for k in range(2):
                u = ((z + 3 - 2 * k) % 4) // 2
                remote(ha.at[b, k], ha.at[b, k], hsend.at[b, k], hrecv.at[b, k], near(dz=1)).wait_recv()
                p[b, u, rows(k)] += ha[b, k]
                remote(p.at[b, u, rows(k)], fu.at[b, k, rows(k)], usend.at[b, k, 1], urecv.at[b, k, 1],
                       near(dz=3 - 2 * k)).start()

    def deliver(src, dst, send, recv, device, same):
        @pl.when(jnp.logical_not(same))
        def _():
            remote(src, dst, send, recv, device).start()

        @pl.when(same)
        def _():
            pltpu.make_async_copy(src, dst, recv).start()

    def delivered(src, dst, send, recv, device, same):
        @pl.when(jnp.logical_not(same))
        def _():
            remote(src, dst, send, recv, device).wait_send()

    def block_of(s, cols):
        return out_ref.at[pl.ds(pl.multiple_of(s * LANES, LANES), LANES), pl.ds(pl.multiple_of(cols, LANES), LANES)]

    def results(b):
        xp, ds, keep, _ = role(b)
        u = z // 2
        s = (y + ds) % 4
        for yh in range(2):
            for cc in range(2):
                yy, zz = yh * 2 + xp % 2, yh * 2 + x // 2
                if keep is not None:
                    yield (fint.at[b, rows(cc), rows(yh)], mb.at[keep, u, c], msend.at[b, yh, cc], mrecv.at[keep, u, c],
                           at(xp, y, zz, cc), (xp == x) & (zz == z) & (cc == c))
                yield (p.at[b, u, rows(yh), rows(cc)], block_of(s, cc * BLOCK + y * LANES), fsend.at[b, yh, cc], frecv,
                       at(x, yy, z, c), yy == y)

    def finish(b):
        _, _, keep, even = role(b)

        @pl.when(even)
        def _():
            for k in range(2):
                for h in range(2):
                    part = fu.at[b, k, rows(k if h else 1 - k)]
                    remote(part, part, usend.at[b, k, h], urecv.at[b, k, h], near(dz=1)).wait_recv()
            value = p[b, z // 2] + fu[b, 0] + fu[b, 1]
            p[b, z // 2] = value
            if keep is not None:
                fint[b] = value.T
            for copy in results(b):
                deliver(*copy)

    def passed(keep):
        xs = (z % 2) * 2 + (x + (1 if keep else 0)) % 2
        ds = jnp.where((xs + 1) % 4 == x, 0, 2) if keep == 2 else 1
        for u in range(2):
            for cc in range(2):
                yy = u * 2 + xs % 2
                yield (mb.at[keep, u, cc], block_of(y, cc * BLOCK + ((y + ds) % 4) * LANES), gsend.at[keep, u, cc], frecv,
                       at(x, yy, z, c), yy == y)

    def pass_on(keep):
        for k, copy in enumerate(passed(keep)):
            remote(copy[0], copy[0], copy[2], mrecv.at[keep, k // 2, k % 2], near(dy=1)).wait_recv()
            deliver(*copy)

    for h in range(2):
        wait_y(2, 1, h)
    turn(1)
    for copy in keeps:
        copy.wait()
    for jy in range(4):
        for h in range(2):
            wait_core(0, jy, h)
    rise(0)
    for h in range(2):
        wait_x(1, 3, h)
        wait_x(3, 3, h)
    turn(0)
    rise(1)
    middle(0)
    for h in range(2):
        wait_x(1, 2, h)
        wait_x(3, 2, h)
        pass_x(3, 2, h)
        pass_x(1, 3, h)
    middle(1)
    for jy in range(4):
        for h in range(2):
            wait_core(1, jy, h)
            wait_core(3, jy, h)
    rise(2)
    rise(3)
    finish(0)
    middle(2)
    middle(3)
    rise(4)
    for j in (3, 1, 2):
        for h in range(2):
            wait_y(j, 2, h)
    turn(2)
    rise(5)
    finish(1)
    finish(2)
    middle(4)
    rise(6)
    finish(3)
    middle(5)
    for jy in range(4):
        for h in range(2):
            wait_x(2, jy, h)
    middle(6)
    for jy in range(4):
        for h in range(2):
            wait_core(2, jy, h)
    rise(7)
    finish(4)
    rise(8)
    middle(7)
    finish(5)
    rise(9)
    middle(8)
    finish(6)
    middle(9)
    pass_on(1)
    finish(7)
    pass_on(2)
    finish(8)
    pass_on(0)
    finish(9)

    for copy in sends:
        copy.wait_send()
    for b in range(len(PRODUCTS)):
        even = role(b)[3]

        @pl.when(even)
        def _():
            for k in range(2):
                remote(p.at[b, 0, rows(k)], ha.at[b, k], hsend.at[b, k], hrecv.at[b, k], near(dz=3 - 2 * k)).wait_send()
            for copy in results(b):
                delivered(*copy)

        @pl.when(jnp.logical_not(even))
        def _():
            for k in range(2):
                for h in range(2):
                    remote(p.at[b, 0, rows(k)], fu.at[b, k, rows(k)], usend.at[b, k, h], urecv.at[b, k, h],
                           near(dz=3 - 2 * k)).wait_send()
    for keep in range(3):
        for copy in passed(keep):
            delivered(*copy)
    pltpu.make_async_copy(out_ref, out_ref, frecv).wait()


def on_device(half_factors):
    d = half_factors.reshape(DEPTH, 4, LANES).transpose(1, 0, 2).reshape(4, 2, HALF, LANES)
    dma = pltpu.SemaphoreType.DMA
    bf16, f32, n = jnp.bfloat16, jnp.float32, len(PRODUCTS)
    return pl.pallas_call(
        kernel,
        out_shape=jax.ShapeDtypeStruct((BLOCK, 2 * BLOCK), f32),
        in_specs=[pl.BlockSpec(memory_space=pl.ANY)],
        out_specs=pl.BlockSpec(memory_space=pl.ANY),
        scratch_shapes=[
            pltpu.VMEM((4, 2, HALF, LANES), bf16),
            pltpu.VMEM((4, 2, 4, 2, HALF, LANES), bf16),
            pltpu.VMEM((3, 2, 2, HALF, LANES), bf16),
            pltpu.VMEM((3, 2, WIDE, DEPTH), bf16),
            pltpu.VMEM((n, 2, WIDE, WIDE), f32),
            pltpu.VMEM((n, 2, LANES, WIDE), f32),
            pltpu.VMEM((n, 2, WIDE, WIDE), f32),
            pltpu.VMEM((n, WIDE, WIDE), f32),
            pltpu.VMEM((3, 2, 2, LANES, LANES), f32),
            dma, dma((2,)), dma((2, 5, 2)), dma((4, 3, 2)), dma((2, 8, 2)), dma((4, 4, 2)), dma((4, 4, 2)), dma((4, 4, 2)),
            dma((n, 2)), dma((n, 2)), dma((n, 2, 2)), dma((n, 2, 2)), dma((n, 2, 2)), dma((n, 2, 2)), dma((3, 2, 2)),
            dma((3, 2, 2)), dma,
        ],
        name="exchange",
        cost_estimate=pl.CostEstimate(flops=2 * 10 * 256 * 512 * 3072, bytes_accessed=4 << 20, transcendentals=0),
        compiler_params=pltpu.CompilerParams(collective_id=0, has_side_effects=True, vmem_limit_bytes=48 << 20),
    )(d)


def solution(mesh):
    return jax.shard_map(
        on_device, mesh=mesh, in_specs=(P("aux", "occ", "ao"),), out_specs=P("ao", ("aux", "occ")), check_vma=False
    )
```

time: 533 us -> 128 us (0.24)
  waiting for transfers between devices: 493 us -> 0 us
  Pallas kernels: 0 us -> 124 us
  matrix products: 22.2 us -> 0 us
  between operations: 13.4 us -> 0.02 us
    reduce_scatter x1 -> x0, waiting for transfers between devices: 324 us -> none  [on_device(): lax.psum_scatter(partial_value, ('aux', 'occ'), scatter_dimension=1, tile...]
    all_gather x1 -> x0, waiting for transfers between devices: 169 us -> none  [on_device(): shard_piece = lax.all_gather(half_factors, 'ao', axis=2, tiled=True)]
    pallas_call x0 -> x1, Pallas kernels: none -> 124 us  [on_device(): pl.pallas_call(kernel, out_shape=jax.ShapeDtypeStruct((BLOCK, 2 * BLOCK),...]
    dot_general x1 -> x0, matrix products: 22.2 us -> none  [contract(): lax.dot_general(local_rows, visitor, (((0,), (0,)), ((), ())), preferred_...]
  transfers between devices with their start and end apart: 2 -> 0, of which waited for: 2 -> 0; matrix products, arithmetic and copies ran while one was open for 0% -> 0% of each run, Pallas kernels for 0% -> 0%
where the time goes in v2:
time: 128 us
  Pallas kernels  124 us (97%)
  local copies, waits for them, and re-layouts  4.02 us (3%)
    pallas_call x1, Pallas kernels, on_device(): pl.pallas_call(kernel, out_shape=jax.ShapeDtypeStruct((BLOCK, 2 * BLOCK),...  124 us
    reshape x2, local copies, waits for them, and re-layouts, on_device(): half_factors.reshape(DEPTH, 4, LANES).transpose(1, 0, 2)  2.7 us

profile of v2, /device:TPU:33, one launch (start us, length us, event | category | flops | bytes accessed | tf_op | source)
XLA Modules:
  0.0 127.6 jit_solution(17650352061988225539)
XLA Ops:
  0.0 2.5 %reshape.6 = bf16[1536,4,128]{2,1,0:T(4,128)(2,1)S(1)} reshape(bf16[384,4,512]{2,1,0:T(4,128)(2,1)} %param.1) | data formatting | bytes 3145728 | tf_op jit(solution)/shard_map/reshape | solution.py:337
  2.5 0.2 copy.2
  2.7 123.6 %exchange.1 = f32[512,1024]{1,0:T(8,128)S(1)} custom-call(bf16[4,2,768,128]{3,2,1,0:T(8,128)(2,1)S(1)} %bitcast.3), custom_call_target="tpu_custom_call" | custom-call | flops 8053063680 | bytes 4194304 | tf_op jit(solution)/shard_map/exchange/pallas_call | solution.py:340
  126.3 1.3 %copy.4 = f32[512,1024]{1,0:T(8,128)} copy(f32[512,1024]{1,0:T(8,128)S(1)} %exchange.1) | data formatting | bytes 4194304

commit v3 on v2

--- a/solution.py
+++ b/solution.py
@@ -14,7 +14,7 @@
 )
 
 
-def kernel(d_ref, out_ref, own, cp, r, rt, p, ha, fu, fint, mb, own_sem, keep_sem, ysend, yrecv, xsend, xrecv, csend, crecv,
+def kernel(d_ref, out_ref, own, cp, r, rt, p, ha, fu, fint, mb, keep_sem, ysend, yrecv, xsend, xrecv, csend, crecv,
            hsend, hrecv, usend, urecv, fsend, msend, mrecv, gsend, frecv):
     ao, z, yl = lax.axis_index("ao"), lax.axis_index("aux"), lax.axis_index("occ")
     c, x, y = ao % 2, (ao // 2) % 4, (ao // 8) * 2 + yl
@@ -29,9 +29,6 @@
         return pltpu.make_async_remote_copy(
             src_ref=src, dst_ref=dst, send_sem=send, recv_sem=recv, device_id=device, device_id_type=MESH
         )
-
-    load = pltpu.make_async_copy(d_ref, own, own_sem)
-    load.start()
 
     here = x // 2 == z % 2
     barrier = pltpu.get_barrier_semaphore()
@@ -45,8 +42,11 @@
                 @pl.when(jnp.logical_not((mx == x) & (mz == z) & (mc == c)))
                 def _():
                     pl.semaphore_signal(barrier, inc=1, device_id=at(mx, y, mz, mc), device_id_type=MESH)
+    for s in range(4):
+        for h in range(2):
+            part = d_ref[pl.ds(h * HALF // 4, HALF // 4), :, pl.ds(s * LANES, LANES)]
+            own[s, h] = part.reshape(HALF, LANES)
     pl.semaphore_wait(barrier, 16 - here.astype(jnp.int32))
-    load.wait()
 
     sends = []
 
@@ -230,20 +230,22 @@
             for copy in results(b):
                 deliver(*copy)
 
-    def passed(keep):
+    def passed(keep, u):
         xs = (z % 2) * 2 + (x + (1 if keep else 0)) % 2
         ds = jnp.where((xs + 1) % 4 == x, 0, 2) if keep == 2 else 1
-        for u in range(2):
-            for cc in range(2):
-                yy = u * 2 + xs % 2
-                yield (mb.at[keep, u, cc], block_of(y, cc * BLOCK + ((y + ds) % 4) * LANES), gsend.at[keep, u, cc], frecv,
-                       at(x, yy, z, c), yy == y)
-
-    def pass_on(keep):
-        for k, copy in enumerate(passed(keep)):
-            remote(copy[0], copy[0], copy[2], mrecv.at[keep, k // 2, k % 2], near(dy=1)).wait_recv()
+        for cc in range(2):
+            yy = u * 2 + xs % 2
+            yield (mb.at[keep, u, cc], block_of(y, cc * BLOCK + ((y + ds) % 4) * LANES), gsend.at[keep, u, cc], frecv,
+                   at(x, yy, z, c), yy == y)
+
+    def pass_on(keep, u):
+        for cc, copy in enumerate(passed(keep, u)):
+            remote(copy[0], copy[0], copy[2], mrecv.at[keep, u, cc], near(dy=1)).wait_recv()
             deliver(*copy)
 
+    for h in range(2):
+        wait_x(1, 3, h)
+        wait_x(3, 3, h)
     for h in range(2):
         wait_y(2, 1, h)
     turn(1)
@@ -252,62 +254,62 @@
     for jy in range(4):
         for h in range(2):
             wait_core(0, jy, h)
+    turn(0)
     rise(0)
-    for h in range(2):
-        wait_x(1, 3, h)
-        wait_x(3, 3, h)
-    turn(0)
     rise(1)
-    middle(0)
     for h in range(2):
         wait_x(1, 2, h)
         wait_x(3, 2, h)
         pass_x(3, 2, h)
         pass_x(1, 3, h)
-    middle(1)
     for jy in range(4):
         for h in range(2):
             wait_core(1, jy, h)
             wait_core(3, jy, h)
     rise(2)
     rise(3)
-    finish(0)
-    middle(2)
-    middle(3)
     rise(4)
     for j in (3, 1, 2):
         for h in range(2):
             wait_y(j, 2, h)
     turn(2)
     rise(5)
+    middle(2)
+    middle(3)
+    rise(6)
+    for jy in range(4):
+        for h in range(2):
+            wait_x(2, jy, h)
+    for jy in range(4):
+        for h in range(2):
+            wait_core(2, jy, h)
+    middle(4)
+    middle(5)
+    rise(7)
+    rise(9)
+    middle(7)
+    middle(9)
+    finish(3)
+    finish(2)
+    middle(6)
+    middle(0)
+    finish(6)
+    finish(0)
+    rise(8)
+    pass_on(1, 1)
+    middle(8)
+    pass_on(1, 0)
+    finish(4)
+    middle(1)
+    finish(5)
     finish(1)
-    finish(2)
-    middle(4)
-    rise(6)
-    finish(3)
-    middle(5)
-    for jy in range(4):
-        for h in range(2):
-            wait_x(2, jy, h)
-    middle(6)
-    for jy in range(4):
-        for h in range(2):
-            wait_core(2, jy, h)
-    rise(7)
-    finish(4)
-    rise(8)
-    middle(7)
-    finish(5)
-    rise(9)
-    middle(8)
-    finish(6)
-    middle(9)
-    pass_on(1)
     finish(7)
-    pass_on(2)
+    finish(9)
+    pass_on(0, 1)
+    pass_on(0, 0)
+    pass_on(2, 0)
+    pass_on(2, 1)
     finish(8)
-    pass_on(0)
-    finish(9)
 
     for copy in sends:
         copy.wait_send()
@@ -328,19 +330,19 @@
                     remote(p.at[b, 0, rows(k)], fu.at[b, k, rows(k)], usend.at[b, k, h], urecv.at[b, k, h],
                            near(dz=3 - 2 * k)).wait_send()
     for keep in range(3):
-        for copy in passed(keep):
-            delivered(*copy)
+        for u in range(2):
+            for copy in passed(keep, u):
+                delivered(*copy)
     pltpu.make_async_copy(out_ref, out_ref, frecv).wait()
 
 
 def on_device(half_factors):
-    d = half_factors.reshape(DEPTH, 4, LANES).transpose(1, 0, 2).reshape(4, 2, HALF, LANES)
     dma = pltpu.SemaphoreType.DMA
     bf16, f32, n = jnp.bfloat16, jnp.float32, len(PRODUCTS)
     return pl.pallas_call(
         kernel,
         out_shape=jax.ShapeDtypeStruct((BLOCK, 2 * BLOCK), f32),
-        in_specs=[pl.BlockSpec(memory_space=pl.ANY)],
+        in_specs=[pl.BlockSpec(memory_space=pltpu.VMEM)],
         out_specs=pl.BlockSpec(memory_space=pl.ANY),
         scratch_shapes=[
             pltpu.VMEM((4, 2, HALF, LANES), bf16),
@@ -352,14 +354,14 @@
             pltpu.VMEM((n, 2, WIDE, WIDE), f32),
             pltpu.VMEM((n, WIDE, WIDE), f32),
             pltpu.VMEM((3, 2, 2, LANES, LANES), f32),
-            dma, dma((2,)), dma((2, 5, 2)), dma((4, 3, 2)), dma((2, 8, 2)), dma((4, 4, 2)), dma((4, 4, 2)), dma((4, 4, 2)),
+            dma((2,)), dma((2, 5, 2)), dma((4, 3, 2)), dma((2, 8, 2)), dma((4, 4, 2)), dma((4, 4, 2)), dma((4, 4, 2)),
             dma((n, 2)), dma((n, 2)), dma((n, 2, 2)), dma((n, 2, 2)), dma((n, 2, 2)), dma((n, 2, 2)), dma((3, 2, 2)),
             dma((3, 2, 2)), dma,
         ],
         name="exchange",
         cost_estimate=pl.CostEstimate(flops=2 * 10 * 256 * 512 * 3072, bytes_accessed=4 << 20, transcendentals=0),
         compiler_params=pltpu.CompilerParams(collective_id=0, has_side_effects=True, vmem_limit_bytes=48 << 20),
-    )(d)
+    )(half_factors)
 
 
 def solution(mesh):

time: 128 us -> 116 us (0.906)
  Pallas kernels: 124 us -> 113 us
  local copies, waits for them, and re-layouts: 4.02 us -> 2.73 us
    pallas_call x1, Pallas kernels: 124 us -> 113 us  [on_device(): pl.pallas_call(kernel, out_shape=jax.ShapeDtypeStruct((BLOCK, 2 * BLOCK),...]
    reshape x2 -> x0, local copies, waits for them, and re-layouts: 2.7 us -> none  [on_device(): half_factors.reshape(DEPTH, 4, LANES).transpose(1, 0, 2)]
    unnamed x1 -> x3, local copies, waits for them, and re-layouts: 1.32 us -> 2.73 us
where the time goes in v3:
time: 116 us; the launch traced here: 115 us
  Pallas kernels  113 us (97%)
  local copies, waits for them, and re-layouts  2.73 us (2%)
    pallas_call x1, Pallas kernels, on_device(): pl.pallas_call(kernel, out_shape=jax.ShapeDtypeStruct((BLOCK, 2 * BLOCK),...  113 us
    unnamed x3, local copies, waits for them, and re-layouts  2.73 us

profile of v3, /device:TPU:33, one launch (start us, length us, event | category | flops | bytes accessed | tf_op | source)
XLA Modules:
  0.0 115.5 jit_solution(11334708063225506790)
XLA Ops:
  0.0 0.0 copy-start
  0.0 1.4 %copy-done = bf16[384,4,512]{2,1,0:T(4,128)(2,1)S(1)} copy-done((bf16[384,4,512]{2,1,0:T(4,128)(2,1)S(1)}, bf16[384,4,512]{2,1,0:T(4,128)(2,1)}, u32[]{:S(2)}) %copy-start) | copy-done | bytes 1572888
  1.4 112.7 %exchange.1 = f32[512,1024]{1,0:T(8,128)S(1)} custom-call(bf16[384,4,512]{2,1,0:T(4,128)(2,1)S(1)} %copy-done), custom_call_target="tpu_custom_call" | custom-call | flops 8053063680 | bytes 4194304 | tf_op jit(solution)/shard_map/exchange/pallas_call | solution.py:342
  114.1 1.3 %copy.3 = f32[512,1024]{1,0:T(8,128)} copy(f32[512,1024]{1,0:T(8,128)S(1)} %exchange.1) | data formatting | bytes 4194304
Async XLA Ops:
  0.0 1.4 %copy-start = (bf16[384,4,512]{2,1,0:T(4,128)(2,1)S(1)}, bf16[384,4,512]{2,1,0:T(4,128)(2,1)}, u32[]{:S(2)}) copy-start(bf16[384,4,512]{2,1,0:T(4,128)(2,1)} %d_ref.1) | copy-start | bytes 4718596

commit v4 on v3

--- a/solution.py
+++ b/solution.py
@@ -9,6 +9,7 @@
 DEPTH, LANES, BLOCK = 1536, 128, 512
 HALF = DEPTH // 2
 WIDE = 2 * LANES
+PARTS = ((0, 168), (168, 88))
 PRODUCTS = (
     (0, 1, 0), (0, 0, None), (1, 1, 1), (3, 1, 1), (1, 0, 2), (3, 2, 2), (0, 2, None), (2, 1, 0), (2, 2, None), (2, 0, None)
 )
@@ -44,8 +45,7 @@
                     pl.semaphore_signal(barrier, inc=1, device_id=at(mx, y, mz, mc), device_id_type=MESH)
     for s in range(4):
         for h in range(2):
-            part = d_ref[pl.ds(h * HALF // 4, HALF // 4), :, pl.ds(s * LANES, LANES)]
-            own[s, h] = part.reshape(HALF, LANES)
+            own[s, h] = d_ref[pl.ds(h * HALF // 4, HALF // 4), :, pl.ds(s * LANES, LANES)].reshape(HALF, LANES)
     pl.semaphore_wait(barrier, 16 - here.astype(jnp.int32))
 
     sends = []
@@ -141,6 +141,15 @@
     def rows(k):
         return pl.ds(k * LANES, LANES)
 
+    def part(k):
+        return pl.ds(*PARTS[k])
+
+    def side(k):
+        return jnp.where((x // 2 + k) % 2 == 0, 3, 1)
+
+    def half(b, k):
+        return ha.at[b, k, pl.ds(0, PARTS[k][1])]
+
     def role(b):
         dx, ds, keep = PRODUCTS[b]
         xp = (x + dx) % 4
@@ -156,21 +165,21 @@
             total = None
             for k in range(2):
                 rhs = jnp.concatenate([cp[xp, cc, 2 * u + k].reshape(DEPTH, LANES) for cc in range(2)], axis=1)
-                part = jnp.dot(rt[ds, k], rhs, preferred_element_type=jnp.float32)
-                total = part if total is None else total + part
+                product = jnp.dot(rt[ds, k], rhs, preferred_element_type=jnp.float32)
+                total = product if total is None else total + product
             p[b, u] = total
 
         @pl.when(even)
         def _():
             for k in range(2):
-                remote(p.at[b, far, rows(k)], ha.at[b, k], hsend.at[b, k], hrecv.at[b, k], near(dz=3 - 2 * k)).start()
+                remote(p.at[b, far, part(k)], half(b, k), hsend.at[b, k], hrecv.at[b, k], near(dz=side(k))).start()
 
         @pl.when(jnp.logical_not(even))
         def _():
             for k in range(2):
-                u = ((z + 3 - 2 * k) % 4) // 2
-                remote(p.at[b, u, rows(1 - k)], fu.at[b, k, rows(1 - k)], usend.at[b, k, 0], urecv.at[b, k, 0],
-                       near(dz=3 - 2 * k)).start()
+                u = ((z + side(k)) % 4) // 2
+                remote(p.at[b, u, part(1 - k)], fu.at[b, k, part(1 - k)], usend.at[b, k, 0], urecv.at[b, k, 0],
+                       near(dz=side(k))).start()
 
     def middle(b):
         _, _, _, even = role(b)
@@ -178,11 +187,11 @@
         @pl.when(jnp.logical_not(even))
         def _():
             for k in range(2):
-                u = ((z + 3 - 2 * k) % 4) // 2
-                remote(ha.at[b, k], ha.at[b, k], hsend.at[b, k], hrecv.at[b, k], near(dz=1)).wait_recv()
-                p[b, u, rows(k)] += ha[b, k]
-                remote(p.at[b, u, rows(k)], fu.at[b, k, rows(k)], usend.at[b, k, 1], urecv.at[b, k, 1],
-                       near(dz=3 - 2 * k)).start()
+                u = ((z + side(k)) % 4) // 2
+                remote(half(b, k), half(b, k), hsend.at[b, k], hrecv.at[b, k], near(dz=1)).wait_recv()
+                p[b, u, part(k)] += ha[b, k, pl.ds(0, PARTS[k][1])]
+                remote(p.at[b, u, part(k)], fu.at[b, k, part(k)], usend.at[b, k, 1], urecv.at[b, k, 1],
+                       near(dz=side(k))).start()
 
     def deliver(src, dst, send, recv, device, same):
         @pl.when(jnp.logical_not(same))
@@ -221,8 +230,8 @@
         def _():
             for k in range(2):
                 for h in range(2):
-                    part = fu.at[b, k, rows(k if h else 1 - k)]
-                    remote(part, part, usend.at[b, k, h], urecv.at[b, k, h], near(dz=1)).wait_recv()
+                    got = fu.at[b, k, part(k if h else 1 - k)]
+                    remote(got, got, usend.at[b, k, h], urecv.at[b, k, h], near(dz=1)).wait_recv()
             value = p[b, z // 2] + fu[b, 0] + fu[b, 1]
             p[b, z // 2] = value
             if keep is not None:
@@ -254,9 +263,10 @@
     for jy in range(4):
         for h in range(2):
             wait_core(0, jy, h)
+    rise(0)
     turn(0)
-    rise(0)
     rise(1)
+    middle(0)
     for h in range(2):
         wait_x(1, 2, h)
         wait_x(3, 2, h)
@@ -266,49 +276,48 @@
         for h in range(2):
             wait_core(1, jy, h)
             wait_core(3, jy, h)
+    rise(3)
     rise(2)
-    rise(3)
     rise(4)
     for j in (3, 1, 2):
         for h in range(2):
             wait_y(j, 2, h)
     turn(2)
+    finish(0)
+    rise(6)
+    middle(3)
+    middle(2)
     rise(5)
-    middle(2)
-    middle(3)
-    rise(6)
     for jy in range(4):
         for h in range(2):
             wait_x(2, jy, h)
     for jy in range(4):
         for h in range(2):
             wait_core(2, jy, h)
-    middle(4)
-    middle(5)
     rise(7)
+    middle(6)
     rise(9)
     middle(7)
+    middle(1)
+    middle(4)
+    finish(3)
+    finish(6)
+    middle(5)
+    finish(2)
     middle(9)
-    finish(3)
-    finish(2)
-    middle(6)
-    middle(0)
-    finish(6)
-    finish(0)
     rise(8)
+    finish(1)
+    pass_on(1, 0)
     pass_on(1, 1)
+    finish(7)
     middle(8)
-    pass_on(1, 0)
+    finish(5)
     finish(4)
-    middle(1)
-    finish(5)
-    finish(1)
-    finish(7)
     finish(9)
+    pass_on(0, 0)
     pass_on(0, 1)
-    pass_on(0, 0)
+    pass_on(2, 1)
     pass_on(2, 0)
-    pass_on(2, 1)
     finish(8)
 
     for copy in sends:
@@ -319,7 +328,7 @@
         @pl.when(even)
         def _():
             for k in range(2):
-                remote(p.at[b, 0, rows(k)], ha.at[b, k], hsend.at[b, k], hrecv.at[b, k], near(dz=3 - 2 * k)).wait_send()
+                remote(p.at[b, 0, part(k)], half(b, k), hsend.at[b, k], hrecv.at[b, k], near(dz=side(k))).wait_send()
             for copy in results(b):
                 delivered(*copy)
 
@@ -327,8 +336,8 @@
         def _():
             for k in range(2):
                 for h in range(2):
-                    remote(p.at[b, 0, rows(k)], fu.at[b, k, rows(k)], usend.at[b, k, h], urecv.at[b, k, h],
-                           near(dz=3 - 2 * k)).wait_send()
+                    sent = p.at[b, 0, part(k if h else 1 - k)]
+                    remote(sent, sent, usend.at[b, k, h], urecv.at[b, k, h], near(dz=side(k))).wait_send()
     for keep in range(3):
         for u in range(2):
             for copy in passed(keep, u):
@@ -350,7 +359,7 @@
             pltpu.VMEM((3, 2, 2, HALF, LANES), bf16),
             pltpu.VMEM((3, 2, WIDE, DEPTH), bf16),
             pltpu.VMEM((n, 2, WIDE, WIDE), f32),
-            pltpu.VMEM((n, 2, LANES, WIDE), f32),
+            pltpu.VMEM((n, 2, PARTS[0][1], WIDE), f32),
             pltpu.VMEM((n, 2, WIDE, WIDE), f32),
             pltpu.VMEM((n, WIDE, WIDE), f32),
             pltpu.VMEM((3, 2, 2, LANES, LANES), f32),

time: 116 us -> 113 us (0.974)
  Pallas kernels: 113 us -> 110 us
    pallas_call x1, Pallas kernels: 113 us -> 110 us  [on_device(): pl.pallas_call(kernel, out_shape=jax.ShapeDtypeStruct((BLOCK, 2 * BLOCK),...]
where the time goes in v4:
time: 113 us
  Pallas kernels  110 us (97%)
  local copies, waits for them, and re-layouts  2.73 us (2%)
    pallas_call x1, Pallas kernels, on_device(): pl.pallas_call(kernel, out_shape=jax.ShapeDtypeStruct((BLOCK, 2 * BLOCK),...  110 us
    unnamed x3, local copies, waits for them, and re-layouts  2.73 us

profile of v4, /device:TPU:33, one launch (start us, length us, event | category | flops | bytes accessed | tf_op | source)
XLA Modules:
  0.0 112.8 jit_solution(18039990605702846376)
XLA Ops:
  0.0 0.0 copy-start
  0.0 1.4 %copy-done = bf16[384,4,512]{2,1,0:T(4,128)(2,1)S(1)} copy-done((bf16[384,4,512]{2,1,0:T(4,128)(2,1)S(1)}, bf16[384,4,512]{2,1,0:T(4,128)(2,1)}, u32[]{:S(2)}) %copy-start) | copy-done | bytes 1572888
  1.4 110.1 %exchange.1 = f32[512,1024]{1,0:T(8,128)S(1)} custom-call(bf16[384,4,512]{2,1,0:T(4,128)(2,1)S(1)} %copy-done), custom_call_target="tpu_custom_call" | custom-call | flops 8053063680 | bytes 4194304 | tf_op jit(solution)/shard_map/exchange/pallas_call | solution.py:351
  111.5 1.3 %copy.3 = f32[512,1024]{1,0:T(8,128)} copy(f32[512,1024]{1,0:T(8,128)S(1)} %exchange.1) | data formatting | bytes 4194304
Async XLA Ops:
  0.0 1.4 %copy-start = (bf16[384,4,512]{2,1,0:T(4,128)(2,1)S(1)}, bf16[384,4,512]{2,1,0:T(4,128)(2,1)}, u32[]{:S(2)}) copy-start(bf16[384,4,512]{2,1,0:T(4,128)(2,1)} %d_ref.1) | copy-start | bytes 4718596

commit v5 on v4

--- a/solution.py
+++ b/solution.py
@@ -15,7 +15,7 @@
 )
 
 
-def kernel(d_ref, out_ref, own, cp, r, rt, p, ha, fu, fint, mb, keep_sem, ysend, yrecv, xsend, xrecv, csend, crecv,
+def kernel(d_ref, out_ref, raw, own, cp, r, rt, p, ha, fu, fint, mb, raw_sem, keep_sem, ysend, yrecv, xsend, xrecv, csend, crecv,
            hsend, hrecv, usend, urecv, fsend, msend, mrecv, gsend, frecv):
     ao, z, yl = lax.axis_index("ao"), lax.axis_index("aux"), lax.axis_index("occ")
     c, x, y = ao % 2, (ao // 2) % 4, (ao // 8) * 2 + yl
@@ -30,6 +30,9 @@
         return pltpu.make_async_remote_copy(
             src_ref=src, dst_ref=dst, send_sem=send, recv_sem=recv, device_id=device, device_id_type=MESH
         )
+
+    load = pltpu.make_async_copy(d_ref, raw, raw_sem)
+    load.start()
 
     here = x // 2 == z % 2
     barrier = pltpu.get_barrier_semaphore()
@@ -43,9 +46,10 @@
                 @pl.when(jnp.logical_not((mx == x) & (mz == z) & (mc == c)))
                 def _():
                     pl.semaphore_signal(barrier, inc=1, device_id=at(mx, y, mz, mc), device_id_type=MESH)
+    load.wait()
     for s in range(4):
         for h in range(2):
-            own[s, h] = d_ref[pl.ds(h * HALF // 4, HALF // 4), :, pl.ds(s * LANES, LANES)].reshape(HALF, LANES)
+            own[s, h] = raw[pl.ds(h * HALF // 4, HALF // 4), :, pl.ds(s * LANES, LANES)].reshape(HALF, LANES)
     pl.semaphore_wait(barrier, 16 - here.astype(jnp.int32))
 
     sends = []
@@ -121,9 +125,8 @@
     for h in range(2):
         wait_y(2, 0, h)
         to_x(piece(0, 2, h), 2, h)
-    for h in range(2):
-        pass_x(3, 0, h)
-        pass_x(1, 1, h)
+    twin = 1 + 2 * (y % 2)
+    other = 4 - twin
 
     def turn(ds):
         for j in range(4):
@@ -155,29 +158,24 @@
         xp = (x + dx) % 4
         return xp, ds, keep, z % 2 == xp // 2
 
-    def rise(b):
+    def rise(b, i):
         xp, ds, _, even = role(b)
-        far = 1 - z // 2
-
-        @pl.loop(0, 2)
-        def _(i):
-            u = (far + i) % 2
-            total = None
+        u = (y // 2 + i) % 2
+        total = None
+        for k in range(2):
+            rhs = jnp.concatenate([cp[xp, cc, 2 * u + k].reshape(DEPTH, LANES) for cc in range(2)], axis=1)
+            product = jnp.dot(rt[ds, k], rhs, preferred_element_type=jnp.float32)
+            total = product if total is None else total + product
+        p[b, u] = total
+
+        @pl.when(even & (u != z // 2))
+        def _():
             for k in range(2):
-                rhs = jnp.concatenate([cp[xp, cc, 2 * u + k].reshape(DEPTH, LANES) for cc in range(2)], axis=1)
-                product = jnp.dot(rt[ds, k], rhs, preferred_element_type=jnp.float32)
-                total = product if total is None else total + product
-            p[b, u] = total
-
-        @pl.when(even)
-        def _():
-            for k in range(2):
-                remote(p.at[b, far, part(k)], half(b, k), hsend.at[b, k], hrecv.at[b, k], near(dz=side(k))).start()
-
-        @pl.when(jnp.logical_not(even))
-        def _():
-            for k in range(2):
-                u = ((z + side(k)) % 4) // 2
+                remote(p.at[b, u, part(k)], half(b, k), hsend.at[b, k], hrecv.at[b, k], near(dz=side(k))).start()
+
+        for k in range(2):
+            @pl.when(jnp.logical_not(even) & (u == ((z + side(k)) % 4) // 2))
+            def _():
                 remote(p.at[b, u, part(1 - k)], fu.at[b, k, part(1 - k)], usend.at[b, k, 0], urecv.at[b, k, 0],
                        near(dz=side(k))).start()
 
@@ -252,73 +250,99 @@
             remote(copy[0], copy[0], copy[2], mrecv.at[keep, u, cc], near(dy=1)).wait_recv()
             deliver(*copy)
 
+    for copy in keeps:
+        copy.wait()
+    for jy in (0, twin):
+        for h in range(2):
+            wait_core(0, jy, h)
     for h in range(2):
         wait_x(1, 3, h)
         wait_x(3, 3, h)
     for h in range(2):
+        pass_x(3, 0, h)
+        pass_x(1, twin, h)
+    for h in range(2):
         wait_y(2, 1, h)
     turn(1)
-    for copy in keeps:
-        copy.wait()
-    for jy in range(4):
+    rise(0, 0)
+    for jy in (other, 2):
         for h in range(2):
             wait_core(0, jy, h)
-    rise(0)
+    rise(0, 1)
     turn(0)
-    rise(1)
+    rise(1, 1)
+    for jy in (0, twin):
+        for h in range(2):
+            wait_core(1, jy, h)
+            wait_core(3, jy, h)
+    rise(3, 0)
+    rise(4, 0)
     middle(0)
+    rise(2, 0)
     for h in range(2):
         wait_x(1, 2, h)
         wait_x(3, 2, h)
         pass_x(3, 2, h)
-        pass_x(1, 3, h)
-    for jy in range(4):
+        pass_x(1, other, h)
+    rise(1, 0)
+    for jy in (other, 2):
         for h in range(2):
             wait_core(1, jy, h)
             wait_core(3, jy, h)
-    rise(3)
-    rise(2)
-    rise(4)
+    rise(2, 1)
+    rise(3, 1)
+    rise(4, 1)
+    finish(0)
     for j in (3, 1, 2):
         for h in range(2):
             wait_y(j, 2, h)
     turn(2)
-    finish(0)
-    rise(6)
+    rise(5, 0)
+    rise(5, 1)
+    middle(2)
+    for jy in (0, twin):
+        for h in range(2):
+            wait_x(2, jy, h)
     middle(3)
-    middle(2)
-    rise(5)
-    for jy in range(4):
+    rise(6, 0)
+    rise(6, 1)
+    for jy in (0, twin):
+        for h in range(2):
+            wait_core(2, jy, h)
+    rise(7, 0)
+    rise(8, 0)
+    for jy in (other, 2):
         for h in range(2):
             wait_x(2, jy, h)
-    for jy in range(4):
+    for jy in (other, 2):
         for h in range(2):
             wait_core(2, jy, h)
-    rise(7)
+    rise(7, 1)
+    rise(8, 1)
+    middle(1)
+    middle(7)
+    rise(9, 0)
+    middle(8)
+    middle(5)
+    finish(3)
+    finish(2)
+    middle(4)
+    finish(1)
+    rise(9, 1)
+    middle(9)
+    finish(7)
+    pass_on(1, 1)
+    pass_on(1, 0)
     middle(6)
-    rise(9)
-    middle(7)
-    middle(1)
-    middle(4)
-    finish(3)
-    finish(6)
-    middle(5)
-    finish(2)
-    middle(9)
-    rise(8)
-    finish(1)
-    pass_on(1, 0)
-    pass_on(1, 1)
-    finish(7)
-    middle(8)
+    finish(8)
     finish(5)
     finish(4)
+    pass_on(0, 1)
+    pass_on(0, 0)
     finish(9)
-    pass_on(0, 0)
-    pass_on(0, 1)
+    finish(6)
     pass_on(2, 1)
     pass_on(2, 0)
-    finish(8)
 
     for copy in sends:
         copy.wait_send()
@@ -351,9 +375,10 @@
     return pl.pallas_call(
         kernel,
         out_shape=jax.ShapeDtypeStruct((BLOCK, 2 * BLOCK), f32),
-        in_specs=[pl.BlockSpec(memory_space=pltpu.VMEM)],
+        in_specs=[pl.BlockSpec(memory_space=pltpu.HBM)],
         out_specs=pl.BlockSpec(memory_space=pl.ANY),
         scratch_shapes=[
+            pltpu.VMEM((DEPTH // 4, 4, BLOCK), bf16),
             pltpu.VMEM((4, 2, HALF, LANES), bf16),
             pltpu.VMEM((4, 2, 4, 2, HALF, LANES), bf16),
             pltpu.VMEM((3, 2, 2, HALF, LANES), bf16),
@@ -363,14 +388,14 @@
             pltpu.VMEM((n, 2, WIDE, WIDE), f32),
             pltpu.VMEM((n, WIDE, WIDE), f32),
             pltpu.VMEM((3, 2, 2, LANES, LANES), f32),
-            dma((2,)), dma((2, 5, 2)), dma((4, 3, 2)), dma((2, 8, 2)), dma((4, 4, 2)), dma((4, 4, 2)), dma((4, 4, 2)),
+            dma, dma((2,)), dma((2, 5, 2)), dma((4, 3, 2)), dma((2, 8, 2)), dma((4, 4, 2)), dma((4, 4, 2)), dma((4, 4, 2)),
             dma((n, 2)), dma((n, 2)), dma((n, 2, 2)), dma((n, 2, 2)), dma((n, 2, 2)), dma((n, 2, 2)), dma((3, 2, 2)),
             dma((3, 2, 2)), dma,
         ],
         name="exchange",
         cost_estimate=pl.CostEstimate(flops=2 * 10 * 256 * 512 * 3072, bytes_accessed=4 << 20, transcendentals=0),
         compiler_params=pltpu.CompilerParams(collective_id=0, has_side_effects=True, vmem_limit_bytes=48 << 20),
-    )(half_factors)
+    )(pltpu.with_memory_space_constraint(half_factors, pltpu.HBM))
 
 
 def solution(mesh):

time: 113 us -> 111 us (0.982)
  local copies, waits for them, and re-layouts: 2.73 us -> 1.32 us
    unnamed x3 -> x1, local copies, waits for them, and re-layouts: 2.73 us -> 1.32 us
where the time goes in v5:
time: 111 us; the launch traced here: 110 us
  Pallas kernels  109 us (98%)
  local copies, waits for them, and re-layouts  1.32 us (1%)
    pallas_call x1, Pallas kernels, on_device(): pl.pallas_call(kernel, out_shape=jax.ShapeDtypeStruct((BLOCK, 2 * BLOCK),...  109 us

profile of v5, /device:TPU:33, one launch (start us, length us, event | category | flops | bytes accessed | tf_op | source)
XLA Modules:
  0.0 110.3 jit_solution(17130945669005677790)
XLA Ops:
  0.0 109.0 %exchange.1 = f32[512,1024]{1,0:T(8,128)S(1)} custom-call(bf16[384,4,512]{2,1,0:T(4,128)(2,1)} %d_ref.1), custom_call_target="tpu_custom_call" | custom-call | flops 8053063680 | bytes 4194304 | tf_op jit(solution)/shard_map/exchange/pallas_call | solution.py:375
  109.0 1.3 %copy.3 = f32[512,1024]{1,0:T(8,128)} copy(f32[512,1024]{1,0:T(8,128)S(1)} %exchange.1) | data formatting | bytes 4194304

commit v6 on v5

--- a/solution.py
+++ b/solution.py
@@ -9,10 +9,12 @@
 DEPTH, LANES, BLOCK = 1536, 128, 512
 HALF = DEPTH // 2
 WIDE = 2 * LANES
-PARTS = ((0, 168), (168, 88))
+PARTS = ((0, 160), (160, 96))
 PRODUCTS = (
     (0, 1, 0), (0, 0, None), (1, 1, 1), (3, 1, 1), (1, 0, 2), (3, 2, 2), (0, 2, None), (2, 1, 0), (2, 2, None), (2, 0, None)
 )
+
+TURNED = 1
 
 
 def kernel(d_ref, out_ref, raw, own, cp, r, rt, p, ha, fu, fint, mb, raw_sem, keep_sem, ysend, yrecv, xsend, xrecv, csend, crecv,
@@ -31,12 +33,19 @@
             src_ref=src, dst_ref=dst, send_sem=send, recv_sem=recv, device_id=device, device_id_type=MESH
         )
 
-    load = pltpu.make_async_copy(d_ref, raw, raw_sem)
-    load.start()
+    quarter = HALF // 4
+    loads = [
+        pltpu.make_async_copy(d_ref.at[pl.ds(h * quarter, quarter)], raw.at[pl.ds(h * quarter, quarter)], raw_sem.at[h])
+        for h in range(2)
+    ]
+    for load in loads:
+        load.start()
 
     here = x // 2 == z % 2
     barrier = pltpu.get_barrier_semaphore()
-    for device in (near(dx=1), near(dx=3), near(dz=1), near(dz=3), near(dc=1), near(dy=1), near(dy=2), near(dy=3)):
+    for device in (near(dx=1), near(dx=3), near(dz=1), near(dz=3), near(dc=1), near(dy=1), near(dy=2), near(dy=3),
+                   near(dz=1, dc=1), near(dz=3, dc=1), at(3 - x, 0, z, c), at(3 - x, 1, z, c), at(3 - x, 2, z, c),
+                   at(3 - x, 3, z, c)):
         pl.semaphore_signal(barrier, inc=1, device_id=device, device_id_type=MESH)
     for bx in range(2):
         for bz in range(2):
@@ -46,11 +55,16 @@
                 @pl.when(jnp.logical_not((mx == x) & (mz == z) & (mc == c)))
                 def _():
                     pl.semaphore_signal(barrier, inc=1, device_id=at(mx, y, mz, mc), device_id_type=MESH)
-    load.wait()
-    for s in range(4):
-        for h in range(2):
-            own[s, h] = raw[pl.ds(h * HALF // 4, HALF // 4), :, pl.ds(s * LANES, LANES)].reshape(HALF, LANES)
-    pl.semaphore_wait(barrier, 16 - here.astype(jnp.int32))
+    def sort(ds, h):
+        s = (y + ds) % 4
+        lanes = pl.ds(pl.multiple_of(s * LANES, LANES), LANES)
+        own[s, h] = raw[pl.ds(h * quarter, quarter), :, lanes].reshape(HALF, LANES)
+
+    loads[0].wait()
+    for ds in (3, 2, 0):
+        sort(ds, 0)
+    loads[1].wait()
+    pl.semaphore_wait(barrier, 22 - here.astype(jnp.int32))
 
     sends = []
 
@@ -95,9 +109,14 @@
 
     keeps = []
     for h in range(2):
+        if h:
+            for ds in (3, 2, 0):
+                sort(ds, h)
         to_y(mine(3, h), piece(0, 0, h), 1, 0, 1, 0, h)
         to_y(mine(2, h), r.at[2, 0, h], 0, 1, 3, 1, h)
         to_x(mine(0, h), 0, h)
+    for h in range(2):
+        sort(1, h)
     for h in range(2):
         to_y(mine(0, h), r.at[0, 0, h], 1, 1, 1, 1, h)
         to_y(mine(1, h), piece(0, 0, h), 0, 0, 3, 0, h)
@@ -192,6 +211,10 @@
                        near(dz=side(k))).start()
 
     def deliver(src, dst, send, recv, device, same):
+        if same is False:
+            remote(src, dst, send, recv, device).start()
+            return
+
         @pl.when(jnp.logical_not(same))
         def _():
             remote(src, dst, send, recv, device).start()
@@ -201,6 +224,10 @@
             pltpu.make_async_copy(src, dst, recv).start()
 
     def delivered(src, dst, send, recv, device, same):
+        if same is False:
+            remote(src, dst, send, recv, device).wait_send()
+            return
+
         @pl.when(jnp.logical_not(same))
         def _():
             remote(src, dst, send, recv, device).wait_send()
@@ -216,8 +243,11 @@
             for cc in range(2):
                 yy, zz = yh * 2 + xp % 2, yh * 2 + x // 2
                 if keep is not None:
-                    yield (fint.at[b, rows(cc), rows(yh)], mb.at[keep, u, c], msend.at[b, yh, cc], mrecv.at[keep, u, c],
-                           at(xp, y, zz, cc), (xp == x) & (zz == z) & (cc == c))
+                    tx, slot = xp, keep
+                    if keep == TURNED:
+                        tx, slot = jnp.where(here, xp, x), jnp.where(here, keep, 3)
+                    yield (fint.at[b, rows(cc), rows(yh)], mb.at[slot, u, c], msend.at[b, yh, cc], mrecv.at[slot, u, c],
+                           at(tx, y, zz, cc), (tx == x) & (zz == z) & (cc == c))
                 yield (p.at[b, u, rows(yh), rows(cc)], block_of(s, cc * BLOCK + y * LANES), fsend.at[b, yh, cc], frecv,
                        at(x, yy, z, c), yy == y)
 
@@ -238,36 +268,45 @@
                 deliver(*copy)
 
     def passed(keep, u):
-        xs = (z % 2) * 2 + (x + (1 if keep else 0)) % 2
-        ds = jnp.where((xs + 1) % 4 == x, 0, 2) if keep == 2 else 1
         for cc in range(2):
-            yy = u * 2 + xs % 2
+            if keep == 3:
+                device, ds, same = at(3 - x, u * 2 + x % 2, z, c), 1, False
+            else:
+                xs = (z % 2) * 2 + (x + (1 if keep else 0)) % 2
+                ds = jnp.where((xs + 1) % 4 == x, 0, 2) if keep == 2 else 1
+                yy = u * 2 + xs % 2
+                device, same = at(x, yy, z, c), yy == y
             yield (mb.at[keep, u, cc], block_of(y, cc * BLOCK + ((y + ds) % 4) * LANES), gsend.at[keep, u, cc], frecv,
-                   at(x, yy, z, c), yy == y)
+                   device, same)
+
+    def when_passed(keep):
+        return here if keep in (TURNED, 3) else True
 
     def pass_on(keep, u):
-        for cc, copy in enumerate(passed(keep, u)):
-            remote(copy[0], copy[0], copy[2], mrecv.at[keep, u, cc], near(dy=1)).wait_recv()
-            deliver(*copy)
-
+        @pl.when(when_passed(keep))
+        def _():
+            for cc, copy in enumerate(passed(keep, u)):
+                remote(copy[0], copy[0], copy[2], mrecv.at[keep, u, cc], near(dy=1)).wait_recv()
+                deliver(*copy)
+
+    for h in range(2):
+        wait_y(2, 1, h)
+    turn(1)
     for copy in keeps:
         copy.wait()
     for jy in (0, twin):
         for h in range(2):
             wait_core(0, jy, h)
+    rise(0, 0)
+    for jy in (other, 2):
+        for h in range(2):
+            wait_core(0, jy, h)
     for h in range(2):
         wait_x(1, 3, h)
         wait_x(3, 3, h)
     for h in range(2):
         pass_x(3, 0, h)
         pass_x(1, twin, h)
-    for h in range(2):
-        wait_y(2, 1, h)
-    turn(1)
-    rise(0, 0)
-    for jy in (other, 2):
-        for h in range(2):
-            wait_core(0, jy, h)
     rise(0, 1)
     turn(0)
     rise(1, 1)
@@ -275,74 +314,76 @@
         for h in range(2):
             wait_core(1, jy, h)
             wait_core(3, jy, h)
+    rise(4, 0)
+    rise(1, 0)
+    middle(0)
     rise(3, 0)
-    rise(4, 0)
-    middle(0)
-    rise(2, 0)
     for h in range(2):
         wait_x(1, 2, h)
         wait_x(3, 2, h)
         pass_x(3, 2, h)
         pass_x(1, other, h)
-    rise(1, 0)
     for jy in (other, 2):
         for h in range(2):
             wait_core(1, jy, h)
             wait_core(3, jy, h)
+    rise(3, 1)
+    rise(2, 0)
     rise(2, 1)
-    rise(3, 1)
     rise(4, 1)
     finish(0)
     for j in (3, 1, 2):
         for h in range(2):
             wait_y(j, 2, h)
     turn(2)
+    for jy in (0, twin):
+        for h in range(2):
+            wait_x(2, jy, h)
+    rise(5, 1)
     rise(5, 0)
-    rise(5, 1)
+    middle(3)
+    for jy in (0, twin):
+        for h in range(2):
+            wait_core(2, jy, h)
     middle(2)
-    for jy in (0, twin):
+    rise(7, 0)
+    for jy in (other, 2):
         for h in range(2):
             wait_x(2, jy, h)
-    middle(3)
     rise(6, 0)
     rise(6, 1)
-    for jy in (0, twin):
-        for h in range(2):
-            wait_core(2, jy, h)
-    rise(7, 0)
-    rise(8, 0)
-    for jy in (other, 2):
-        for h in range(2):
-            wait_x(2, jy, h)
+    rise(9, 0)
     for jy in (other, 2):
         for h in range(2):
             wait_core(2, jy, h)
     rise(7, 1)
+    rise(9, 1)
+    middle(7)
+    rise(8, 0)
     rise(8, 1)
-    middle(1)
-    middle(7)
-    rise(9, 0)
-    middle(8)
-    middle(5)
+    middle(9)
     finish(3)
     finish(2)
+    pass_on(3, 0)
     middle(4)
-    finish(1)
-    rise(9, 1)
-    middle(9)
+    middle(5)
     finish(7)
+    middle(1)
+    middle(8)
+    middle(6)
+    pass_on(3, 1)
+    finish(9)
+    pass_on(0, 0)
+    pass_on(0, 1)
+    pass_on(1, 0)
     pass_on(1, 1)
-    pass_on(1, 0)
-    middle(6)
-    finish(8)
     finish(5)
     finish(4)
-    pass_on(0, 1)
-    pass_on(0, 0)
-    finish(9)
+    finish(1)
+    finish(8)
     finish(6)
+    pass_on(2, 0)
     pass_on(2, 1)
-    pass_on(2, 0)
 
     for copy in sends:
         copy.wait_send()
@@ -362,10 +403,12 @@
                 for h in range(2):
                     sent = p.at[b, 0, part(k if h else 1 - k)]
                     remote(sent, sent, usend.at[b, k, h], urecv.at[b, k, h], near(dz=side(k))).wait_send()
-    for keep in range(3):
+    for keep in range(4):
         for u in range(2):
-            for copy in passed(keep, u):
-                delivered(*copy)
+            @pl.when(when_passed(keep))
+            def _():
+                for copy in passed(keep, u):
+                    delivered(*copy)
     pltpu.make_async_copy(out_ref, out_ref, frecv).wait()
 
 
@@ -387,10 +430,10 @@
             pltpu.VMEM((n, 2, PARTS[0][1], WIDE), f32),
             pltpu.VMEM((n, 2, WIDE, WIDE), f32),
             pltpu.VMEM((n, WIDE, WIDE), f32),
-            pltpu.VMEM((3, 2, 2, LANES, LANES), f32),
-            dma, dma((2,)), dma((2, 5, 2)), dma((4, 3, 2)), dma((2, 8, 2)), dma((4, 4, 2)), dma((4, 4, 2)), dma((4, 4, 2)),
-            dma((n, 2)), dma((n, 2)), dma((n, 2, 2)), dma((n, 2, 2)), dma((n, 2, 2)), dma((n, 2, 2)), dma((3, 2, 2)),
-            dma((3, 2, 2)), dma,
+            pltpu.VMEM((4, 2, 2, LANES, LANES), f32),
+            dma((2,)), dma((2,)), dma((2, 5, 2)), dma((4, 3, 2)), dma((2, 8, 2)), dma((4, 4, 2)), dma((4, 4, 2)), dma((4, 4, 2)),
+            dma((n, 2)), dma((n, 2)), dma((n, 2, 2)), dma((n, 2, 2)), dma((n, 2, 2)), dma((n, 2, 2)), dma((4, 2, 2)),
+            dma((4, 2, 2)), dma,
         ],
         name="exchange",
         cost_estimate=pl.CostEstimate(flops=2 * 10 * 256 * 512 * 3072, bytes_accessed=4 << 20, transcendentals=0),

time: 111 us -> 110 us (level)
  no operation moved by 1% of the time
where the time goes in v6:
time: 110 us
  Pallas kernels  109 us (99%)
  local copies, waits for them, and re-layouts  1.32 us (1%)
    pallas_call x1, Pallas kernels, on_device(): pl.pallas_call(kernel, out_shape=jax.ShapeDtypeStruct((BLOCK, 2 * BLOCK),...  109 us

profile of v6, /device:TPU:33, one launch (start us, length us, event | category | flops | bytes accessed | tf_op | source)
XLA Modules:
  0.0 109.9 jit_solution(6499924003608266274)
XLA Ops:
  0.0 108.6 %exchange.1 = f32[512,1024]{1,0:T(8,128)S(1)} custom-call(bf16[384,4,512]{2,1,0:T(4,128)(2,1)} %d_ref.1), custom_call_target="tpu_custom_call" | custom-call | flops 8053063680 | bytes 4194304 | tf_op jit(solution)/shard_map/exchange/pallas_call | solution.py:418
  108.6 1.3 %copy.3 = f32[512,1024]{1,0:T(8,128)} copy(f32[512,1024]{1,0:T(8,128)S(1)} %exchange.1) | data formatting | bytes 4194304
